TPU v7x, 32 devices: a whole 2x2x4 slice. The times are simulated.
32 devices in a mesh: ep: 2 (over x), kv: 16 (over z, y, core).
Axes of the slice: x: 2, y: 2, z: 4, core: 2. Of those that a mesh axis runs over, the one named last changes fastest.
Arguments:
- queries: bfloat16 [32, 1536], P(('ep', 'kv'))
- key_cache_pages: bfloat16 [512, 64, 512], P(('ep', 'kv'))
- value_cache_pages: bfloat16 [512, 64, 512], P(('ep', 'kv')), may hold values from -5 to 5
- page_table: int32 [32, 65], replicated, may hold values from 0 to 511, as said below
- lengths: int32 [32], replicated, may hold values from 2 to 32768, as said below
- sink_head_logits: float32 [24], replicated, may hold values from -1 to 5
- output_weight: bfloat16 [1536, 1536], replicated, may hold values from -0.15625 to 0.15625
- decode_stream: bfloat16 [32, 1536], P(('ep', 'kv')), may hold values from -6 to 6
- prefill_stream: bfloat16 [4064, 1536], P(('ep', 'kv')), may hold values from -6 to 6
- norm_gain: float32 [1536], replicated, may hold values from 0.1 to 1.9
- expert_gate: bfloat16 [16, 1536, 512], P('kv'), may hold values from -0.15625 to 0.15625
- expert_up: bfloat16 [16, 1536, 512], P('kv'), may hold values from -0.15625 to 0.15625
- expert_down: bfloat16 [16, 512, 1536], P('kv'), may hold values from -0.25 to 0.25
- route_ids: int32 [4096, 8], P(('ep', 'kv')), may hold values from 0 to 15, all different within a row; in each aligned block of 128 rows (0 to 127, 128 to 255, ...) at most 96 rows name the same one
- route_gates: float32 [4096, 8], P(('ep', 'kv')), may hold values from 0.03 to 0.6
Outputs:
- layer_out: bfloat16 [4096, 1536], P(('ep', 'kv'))
Inputs may be any that keep to these rules, and one draw needn't show every extreme that they name: In each aligned block of 16 requests, 1 request, which ones drawn from the seed, have lengths of 4096 or more; the others have lengths of at most 512. `page_table`: no two live slots name the same page. Every slot of a request in aligned block g of 16 requests names a page among g * 16 * 16 to (g + 1) * 16 * 16 - 1. `route_ids`: every row names 8 different experts; among the 128 rows of one device no expert is named by more than 96 rows.
All inputs are finite; a program needn't handle non-finite values.
Results may differ from a plain program's by a relative error of at most 0.0053.
Values may be sent and summed in bfloat16 or wider, within the bound.
A program may use at most 128 MiB of HBM per device.

v0:
```python
import jax
import jax.numpy as jnp
from jax import lax
from jax.sharding import PartitionSpec as P

QUERY_HEADS = 24
KEY_VALUE_HEADS = 8
HEAD_WIDTH = 64
TOPK = 8
WINDOW = 4096


lowest = -1e30


def joined(shard, axis, combine):
    everything = jax.tree.map(lambda part: lax.all_gather(part, axis), shard)
    leading = jax.tree.map(lambda part: part[0], everything)

    def step(k, so_far):
        return combine(so_far, jax.tree.map(lambda part: part[k], everything))

    return lax.fori_loop(1, lax.axis_size(axis), step, leading)


def merge_partials(first_part, second_part):
    max_first, total_first, out_first = first_part
    max_second, total_second, out_second = second_part
    highest = jnp.maximum(max_first, max_second)
    weight_first = jnp.exp(max_first - highest)
    weight_second = jnp.exp(max_second - highest)
    merged_total = total_first * weight_first + total_second * weight_second
    merged_out = out_first * jnp.repeat(weight_first, HEAD_WIDTH, axis=1) + out_second * jnp.repeat(
        weight_second, HEAD_WIDTH, axis=1
    )
    return (highest, merged_total, merged_out)


def rms_rows(stream):
    widened = stream.astype(jnp.float32)
    return widened * lax.rsqrt(jnp.mean(widened * widened, axis=-1, keepdims=True) + 1e-06)


def on_device(
    queries,
    key_cache_pages,
    value_cache_pages,
    page_table,
    lengths,
    sink_head_logits,
    output_weight,
    decode_stream,
    prefill_stream,
    norm_gain,
    expert_gate,
    expert_up,
    expert_down,
    route_ids,
    route_gates,
):
    device_index = lax.axis_index(("ep", "kv"))
    group_index = lax.axis_index("ep")
    member_index = lax.axis_index("kv")
    request_count = lax.axis_size("kv")
    local_pool_index = key_cache_pages.shape[0]
    page_length = key_cache_pages.shape[1]
    win_slots = page_table.shape[1]
    group_width = QUERY_HEADS // KEY_VALUE_HEADS
    score_scale = HEAD_WIDTH ** (-0.5)
    query_rows_full = lax.all_gather(queries, "kv", axis=0, tiled=True)
    group_first = group_index * request_count
    group_table = lax.dynamic_slice_in_dim(page_table, group_first, request_count, 0)
    group_lengths = lax.dynamic_slice_in_dim(lengths, group_first, request_count, 0)
    window_start = jnp.maximum(group_lengths - WINDOW, 0)
    first_page = window_start // page_length
    slot_index = jnp.arange(win_slots, dtype=jnp.int32)
    live_slot = (first_page[:, None] + slot_index[None, :]) * page_length < group_lengths[:, None]
    local_id = group_table - device_index * local_pool_index
    mine = live_slot & (local_id >= 0) & (local_id < local_pool_index)
    target = jnp.where(mine, local_id, local_pool_index).reshape(-1)
    request_grid = jnp.broadcast_to(
        jnp.arange(request_count, dtype=jnp.int32)[:, None], (request_count, win_slots)
    ).reshape(-1)
    slot_grid = jnp.broadcast_to(slot_index[None, :], (request_count, win_slots)).reshape(-1)
    page_request = (
        jnp.full((local_pool_index,), request_count, jnp.int32)
        .at[target]
        .set(request_grid, mode="drop")
    )
    page_slot = jnp.zeros((local_pool_index,), jnp.int32).at[target].set(slot_grid, mode="drop")
    page_used = page_request < request_count
    clamped_request = jnp.minimum(page_request, request_count - 1)
    page_first = (first_page[clamped_request] + page_slot) * page_length
    positions = page_first[:, None] + jnp.arange(page_length, dtype=jnp.int32)[None, :]
    in_window = (
        page_used[:, None]
        & (positions >= window_start[clamped_request][:, None])
        & (positions < group_lengths[clamped_request][:, None])
    )
    queries_of_page = query_rows_full[clamped_request].reshape(
        local_pool_index, KEY_VALUE_HEADS, group_width, HEAD_WIDTH
    )
    key_pieces = key_cache_pages.reshape(local_pool_index, page_length, KEY_VALUE_HEADS, HEAD_WIDTH)
    value_pieces = value_cache_pages.reshape(
        local_pool_index, page_length, KEY_VALUE_HEADS, HEAD_WIDTH
    )
    scores = (
        jnp.einsum(
            "pgqd,ptgd->pgqt", queries_of_page, key_pieces, preferred_element_type=jnp.float32
        )
        * score_scale
    )
    mask_full = in_window[:, None, None, :]
    scores = jnp.where(mask_full, scores, lowest)
    slot_max = jnp.max(scores, axis=-1)
    weights = jnp.where(mask_full, jnp.exp(scores - slot_max[..., None]), 0.0).astype(jnp.bfloat16)
    slot_total = jnp.sum(weights.astype(jnp.float32), axis=-1).reshape(
        local_pool_index, QUERY_HEADS
    )
    slot_out = jnp.einsum(
        "pgqt,ptgd->pgqd", weights, value_pieces, preferred_element_type=jnp.float32
    ).reshape(local_pool_index, QUERY_HEADS, HEAD_WIDTH)
    slot_max = jnp.where(
        page_used[:, None], slot_max.reshape(local_pool_index, QUERY_HEADS), lowest
    )
    owner = (page_request[None, :] == jnp.arange(request_count, dtype=jnp.int32)[:, None])[
        :, :, None
    ]
    request_max = jnp.max(jnp.where(owner, slot_max[None], lowest), axis=1)
    rescale = jnp.where(owner, jnp.exp(slot_max[None] - request_max[:, None]), 0.0)
    request_total = jnp.sum(rescale * slot_total[None], axis=1)
    request_out = jnp.einsum("rph,phd->rhd", rescale, slot_out).reshape(
        request_count, QUERY_HEADS * HEAD_WIDTH
    )
    merged_max, merged_total, merged_out = joined(
        (request_max, request_total, request_out), "kv", merge_partials
    )
    own_max = lax.dynamic_slice_in_dim(merged_max, member_index, 1, 0)
    own_total = lax.dynamic_slice_in_dim(merged_total, member_index, 1, 0)
    own_out = lax.dynamic_slice_in_dim(merged_out, member_index, 1, 0)
    sink_logit_row = sink_head_logits[None, :]
    ceiling = jnp.maximum(own_max, sink_logit_row)
    keep_factor = jnp.exp(own_max - ceiling)
    denominator = own_total * keep_factor + jnp.exp(sink_logit_row - ceiling)
    attended = (own_out * jnp.repeat(keep_factor / denominator, HEAD_WIDTH, axis=1)).astype(
        jnp.bfloat16
    )
    decode_hidden = (
        decode_stream.astype(jnp.float32)
        + jnp.dot(attended, output_weight, preferred_element_type=jnp.float32)
    ).astype(jnp.bfloat16)
    gain_row = norm_gain[None, :]
    normed_prefill = (rms_rows(prefill_stream) * gain_row).astype(jnp.bfloat16)
    normed_decode = (rms_rows(decode_hidden) * gain_row).astype(jnp.bfloat16)
    mixed_rows = jnp.concatenate([prefill_stream, decode_hidden], axis=0)
    residual = mixed_rows.astype(jnp.float32)
    row_count = mixed_rows.shape[0]
    width = mixed_rows.shape[1]
    expert_count = lax.axis_size("kv")
    capacity = min(row_count, 3 * row_count * TOPK // (2 * expert_count))
    pair_expert = route_ids.reshape(-1)
    onehot = (pair_expert[:, None] == jnp.arange(expert_count, dtype=jnp.int32)[None, :]).astype(
        jnp.int32
    )
    pair_rank = jnp.sum((jnp.cumsum(onehot, axis=0) - onehot) * onehot, axis=1)
    pair_slot = pair_expert * capacity + pair_rank
    pair_row = jnp.arange(row_count * TOPK, dtype=jnp.int32) // TOPK
    slot_row = (
        jnp.full((expert_count * capacity,), row_count, jnp.int32).at[pair_slot].set(pair_row)
    )
    normed = jnp.concatenate([normed_prefill, normed_decode], axis=0)
    extended = jnp.concatenate([normed, jnp.zeros((1, width), jnp.bfloat16)], axis=0)
    outgoing = extended[slot_row].reshape(expert_count, capacity, width)
    slot_block = lax.all_to_all(outgoing, "kv", split_axis=0, concat_axis=0, tiled=True)
    gate_part = jnp.einsum(
        "scd,df->scf", slot_block, expert_gate[0], preferred_element_type=jnp.float32
    )
    up_part = jnp.einsum(
        "scd,df->scf", slot_block, expert_up[0], preferred_element_type=jnp.float32
    )
    hidden = (jax.nn.silu(gate_part) * up_part).astype(jnp.bfloat16)
    processed = jnp.einsum(
        "scf,fd->scd", hidden, expert_down[0], preferred_element_type=jnp.float32
    ).astype(jnp.bfloat16)
    returned = lax.all_to_all(processed, "kv", split_axis=0, concat_axis=0, tiled=True).reshape(
        expert_count * capacity, width
    )
    pair_values = returned[pair_slot]
    weighted = (
        pair_values.reshape(row_count, TOPK, width).astype(jnp.float32) * route_gates[:, :, None]
    )
    combined = jnp.sum(weighted, axis=1)
    return (residual + combined).astype(jnp.bfloat16)


def solution(mesh):
    in_specs = (
        P(("ep", "kv"), None),
        P(("ep", "kv"), None, None),
        P(("ep", "kv"), None, None),
        P(),
        P(),
        P(),
        P(),
        P(("ep", "kv"), None),
        P(("ep", "kv"), None),
        P(),
        P("kv", None, None),
        P("kv", None, None),
        P("kv", None, None),
        P(("ep", "kv"), None),
        P(("ep", "kv"), None),
    )
    out_specs = P(("ep", "kv"), None)
    return jax.shard_map(
        on_device, mesh=mesh, in_specs=in_specs, out_specs=out_specs, check_vma=False
    )
```

profile of v0, /device:TPU:13, one launch (start us, length us, event | category | flops | bytes accessed | tf_op | source)
XLA Modules:
  0.0 396.2 jit_solution(12079475339717835462)
XLA Ops:
  6.5 0.9 add_maximum_fusion
  7.4 0.8 fusion.36
  8.4 6.4 %scatter_custom_fusion = s32[16]{0:T(128)S(1)} fusion(s32[1040]{0:T(1024)S(1)} %fusion.43, s32[1040]{0:T(1024)S(1)} %reshape.312, s32[]{:T(128)} %constant.108.clone.1), kind=kCustom, calls=%fused_computation.114 | custom fusion | bytes 68 | tf_op jit(solution)/shard_map/scatter | solution.py:88
  14.9 0.7 gather_fusion
  15.6 0.7 gather_fusion.2
  16.4 6.4 %scatter_custom_fusion.1 = s32[16]{0:T(128)S(1)} fusion(s32[1040]{0:T(1024)S(1)} %fusion.43, s32[1040]{0:T(1024)S(1)} %reshape.320, s32[]{:T(128)} %constant.107.clone.1), kind=kCustom, calls=%fused_computation.111 | custom fusion | bytes 68 | tf_op jit(solution)/shard_map/scatter | solution.py:90
  22.8 0.7 gather_fusion.1
  23.5 16.1 %all-gather.2 = bf16[16,1,1536]{2,1,0:T(2,128)(2,1)S(1)} all-gather(bf16[1,1,1536]{2,1,0:T(2,128)(2,1)} %bitcast.96), channel_id=1, replica_groups=mesh['ep'=2,'kv'=16] {'kv'}, dimensions={0}, use_global_device_ids=true | all-gather | bytes 52224 | tf_op jit(solution)/shard_map/all_gather | solution.py:70
  39.6 0.6 gather_fusion.3
  40.4 2.1 reshape.251
  42.5 3.9 reshape.253
  46.5 2.9 fusion.63
  49.5 2.4 fusion.5
  52.1 0.2 convolution_bitcast_fusion
  52.4 0.7 all_gather_reshape.3
  53.5 0.4 convert_reduce_fusion
  54.4 21.7 %all-gather.1 = f32[256,24]{1,0:T(8,128)S(1)} all-gather(f32[16,24]{1,0:T(8,128)S(1)} %copy.72), channel_id=3, replica_groups=mesh['ep'=2,'kv'=16] {'kv'}, dimensions={0}, use_global_device_ids=true | all-gather | bytes 26112 | tf_op jit(solution)/shard_map/all_gather | solution.py:17
  76.1 18.0 %all-gather = f32[256,24]{1,0:T(8,128)S(1)} all-gather(f32[16,24]{1,0:T(8,128)S(1)} %copy.70), channel_id=2, replica_groups=mesh['ep'=2,'kv'=16] {'kv'}, dimensions={0}, use_global_device_ids=true | all-gather | bytes 26112 | tf_op jit(solution)/shard_map/all_gather | solution.py:17
  94.1 4.5 %reduce-window.6 = s32[16,8,128]{2,1,0:T(8,128)S(1)} reduce-window(s32[16,8,128]{2,1,0:T(8,128)S(1)} %fusion.31, s32[]{:T(128)} %constant.107.clone.1), window={size=1x1x128 pad=0_0x0_0x127_0}, to_apply=%region_10.11 | reduce-window | flops 2080768 | bytes 131076 | tf_op jit(solution)/shard_map/reduce-window
  99.3 4.3 %scatter_custom_fusion.2 = s32[1536]{0:T(1024)S(1)} fusion(s32[1024]{0:T(1024)S(1)} %bitcast.94, s32[1024]{0:T(1024)S(1)} %add_select_fusion, s32[]{:T(128)} %constant.127.clone.1), kind=kCustom, calls=%fused_computation.90 | custom fusion | bytes 6148 | tf_op jit(solution)/shard_map/scatter | solution.py:169
  104.0 0.9 slice_bitcast_fusion
  105.0 21.4 %while.19 = (s32[]{:T(128)}, f32[16,24]{1,0:T(8,128)S(1)}, f32[16,24]{1,0:T(8,128)S(1)}, f32[16,1536]{1,0:T(8,128)S(1)}, f32[16,16,24]{2,1,0:T(8,128)S(1)}, /*in...) while((s32[]{:T(128)}, f32[16,24]{1,0:T(8,128)S(1)}, ...), condition=%wide.region_7.8_spmd, body=%wide.region_6.7_spmd.sunk | while | flops 76037 | bytes 1096855 | solution.py:23
  105.4 0.9 fusion.72
  106.9 0.9 fusion.72
  108.3 0.9 fusion.72
  109.7 0.9 fusion.72
  111.1 0.9 fusion.72
  112.6 0.9 fusion.72
  114.0 0.9 fusion.72
  115.4 0.9 fusion.72
  116.8 0.9 fusion.72
  118.3 0.9 fusion.72
  119.7 0.9 fusion.72
  121.1 0.9 fusion.72
  122.6 0.9 fusion.72
  124.0 0.9 fusion.72
  125.4 0.9 fusion.72
  126.5 3.7 multiply_reduce_fusion.1
  131.1 6.2 %gather_fusion.4 = bf16[1536,1536]{1,0:T(8,128)(2,1)} fusion(bf16[129,1536]{1,0:T(8,128)(2,1)S(1)} %maximum_maximum_fusion, s32[2048]{0:T(1024)S(1)} %pad_clamp_fusion), kind=kCustom, calls=%fused_computation.4 | custom fusion | bytes 9443328 | tf_op jit(solution)/shard_map/gather | solution.py:173
  137.3 111.5 %all_to_all.10 = bf16[16,96,1536]{2,1,0:T(8,128)(2,1)S(1)} all-to-all(bf16[16,96,1536]{2,1,0:T(8,128)(2,1)} %bitcast.86), channel_id=1, replica_groups=mesh['ep'=2,'kv'=16] {'kv'}, dimensions={0} | all-to-all | bytes 9437184 | tf_op jit(solution)/shard_map/all_to_all | solution.py:174
  248.8 2.2 copy-done.1
  251.0 4.2 %fusion.10 = f32[16,96,512]{2,1,0:T(8,128)} fusion(bf16[16,96,1536]{2,1,0:T(8,128)(2,1)S(1)} %all_to_all.10, bf16[1,1536,512]{2,1,0:T(8,128)(2,1)S(1)} %copy-done.9), kind=kOutput, calls=%fused_computation.28 | convolution fusion | flops 2415919104 | bytes 9437184 | tf_op jit(solution)/shard_map/scd,df->scf/dot_general | solution.py:178
  255.2 9.6 %convolution_convert_fusion = bf16[16,96,1536]{2,1,0:T(8,128)(2,1)} fusion(bf16[1,512,1536]{2,1,0:T(8,128)(2,1)S(1)} %copy-done, f32[16,96,512]{2,1,0:T(8,128)} %fusion.10, bf16[16,96,1536]{2,1,0:T(8,128)(2,1)} %copy-done.1, bf16[1,1536,512]{2,1,0:T(8,128)(2,1)} %param.27), kind=kOutput, calls=%fused_computation.19 | convolution fusion | flops 4838916096 | bytes 15728640 | tf_op jit(solution)/shard_map/scf,fd->scd/dot_general | solution.py:182
  264.8 5.0 %all-to-all-start.1 = ((bf16[16,96,1536]{2,1,0:T(8,128)(2,1)}), bf16[16,96,1536]{2,1,0:T(8,128)(2,1)}, u32[]{:S(2)}, u32[]{:S(2)}) async-start(bf16[16,96,1536]{2,1,0:T(8,128)(2,1)} %convolution_convert_fusion), calls=%async_computation.1 | async-start | bytes 9437184 | tf_op jit(solution)/shard_map/all_to_all | solution.py:185
  270.0 103.6 %all-to-all-done.1 = bf16[16,96,1536]{2,1,0:T(8,128)(2,1)} async-done(((bf16[16,96,1536]{2,1,0:T(8,128)(2,1)}), bf16[16,96,1536]{2,1,0:T(8,128)(2,1)}, u32[]{:S(2)}, u32[]{:S(2)}) %all-to-all-start.1) | async-done | bytes 4718624 | tf_op jit(solution)/shard_map/all_to_all | solution.py:185
  373.6 10.2 %gather_fusion.5 = bf16[1024,1536]{1,0:T(8,128)(2,1)} fusion(bf16[1536,1536]{1,0:T(8,128)(2,1)} %bitcast.22, s32[1024]{0:T(1024)S(1)} %broadcast_clamp_fusion), kind=kCustom, calls=%fused_computation.5 | custom fusion | bytes 6295552 | tf_op jit(solution)/shard_map/gather | solution.py:188
  383.8 4.7 %fusion.3 = f32[128,1536]{1,0:T(8,128)S(1)} fusion(bf16[1024,1536]{1,0:T(8,128)(2,1)} %gather_fusion.5, f32[128,8]{1,0:T(8,128)S(1)} %copy.85), kind=kLoop, calls=%fused_computation.18 | loop fusion | flops 4521984 | bytes 3936256 | tf_op jit(solution)/shard_map/reduce_sum | solution.py:192
  388.5 0.8 add_convert_fusion
  (154 shorter events, 10.0 us)
Async XLA Ops:
  6.5 248.7 %copy-start = (bf16[1,512,1536]{2,1,0:T(8,128)(2,1)S(1)}, bf16[1,512,1536]{2,1,0:T(8,128)(2,1)}, u32[]{:S(2)}) copy-start(bf16[1,512,1536]{2,1,0:T(8,128)(2,1)} %param.29) | copy-start | bytes 4718596
  6.5 33.8 %copy-start.3 = (bf16[16,64,512]{2,1,0:T(8,128)(2,1)S(1)}, bf16[16,64,512]{2,1,0:T(8,128)(2,1)}, u32[]{:S(2)}) copy-start(bf16[16,64,512]{2,1,0:T(8,128)(2,1)} %param.18) | copy-start | bytes 3145732
  6.5 97.5 %all-gather.5.cloned.1.call-start = ((), (), s32[]{:S(2)}) async-start(), calls=%async_computation.2 | async-start | bytes 1671168 | tf_op jit(solution)/shard_map/all_gather | solution.py:17
  46.5 6.8 %copy-start.5 = (s32[128,8]{0,1:T(8,128)S(1)}, s32[128,8]{0,1:T(8,128)}, u32[]{:S(2)}) copy-start(s32[128,8]{0,1:T(8,128)} %param.30) | copy-start | bytes 12292
  49.4 54.2 %copy-start.2 = (bf16[127,1536]{1,0:T(8,128)(2,1)S(1)}, bf16[127,1536]{1,0:T(8,128)(2,1)}, u32[]{:S(2)}) copy-start(bf16[127,1536]{1,0:T(8,128)(2,1)} %param.25) | copy-start | bytes 1170436
  49.4 54.4 %copy-start.4 = (f32[1536]{0:T(1024)S(1)}, f32[1536]{0:T(1024)}, u32[]{:S(2)}) copy-start(f32[1536]{0:T(1024)} %param.26) | copy-start | bytes 18436
  104.9 21.4 %copy-start.8 = (f32[24]{0:T(128)S(1)}, f32[24]{0:T(128)}, u32[]{:S(2)}) copy-start(f32[24]{0:T(128)} %param.22) | copy-start | bytes 292
  104.9 21.6 %copy-start.6 = (bf16[1,1536]{1,0:T(2,128)(2,1)S(1)}, bf16[1,1536]{1,0:T(2,128)(2,1)}, u32[]{:S(2)}) copy-start(bf16[1,1536]{1,0:T(2,128)(2,1)} %param.24) | copy-start | bytes 9220
  137.3 113.7 %copy-start.9 = (bf16[1,1536,512]{2,1,0:T(8,128)(2,1)S(1)}, bf16[1,1536,512]{2,1,0:T(8,128)(2,1)}, u32[]{:S(2)}) copy-start(bf16[1,1536,512]{2,1,0:T(8,128)(2,1)} %param.28) | copy-start | bytes 4718596
  248.8 2.2 copy-start.1
  264.8 5.0 %copy-start.7 = (f32[128,8]{0,1:T(8,128)S(1)}, f32[128,8]{0,1:T(8,128)}, u32[]{:S(2)}) copy-start(f32[128,8]{0,1:T(8,128)} %param.31) | copy-start | bytes 12292
  264.8 108.7 %all-to-all-start.1 = ((bf16[16,96,1536]{2,1,0:T(8,128)(2,1)}), bf16[16,96,1536]{2,1,0:T(8,128)(2,1)}, u32[]{:S(2)}, u32[]{:S(2)}) async-start(bf16[16,96,1536]{2,1,0:T(8,128)(2,1)} %convolution_convert_fusion), calls=%async_computation.1 | async-start | bytes 9437184 | tf_op jit(solution)/shard_map/all_to_all | solution.py:185
Sparse Core Ops, SparseCore 0:
  53.3 41.7 all-gather.4
where the time goes:
time: 397 us; the launch traced here: 396 us
  blocking collectives  167 us (42%)
  waiting for transfers between devices  104 us (26%)
  local copies, waits for them, and re-layouts  54.5 us (14%)
  other arithmetic  27.7 us (7%)
  matrix products  22.9 us (6%)
  between operations  14.4 us (4%)
  starting transfers between devices  5.04 us (1%)
    all_to_all x1, blocking collectives, on_device(): lax.all_to_all(outgoing, 'kv', split_axis=0, concat_axis=0, tiled=True)  112 us
    all_to_all x1, waiting for transfers between devices, on_device(): lax.all_to_all(processed, 'kv', split_axis=0, concat_axis=0, tiled=True)  104 us
    all_gather x2, blocking collectives, joined(): everything = jax.tree.map(lambda part: lax.all_gather(part, axis), shard)  39.7 us
    all_gather x1, blocking collectives, on_device(): query_rows_full = lax.all_gather(queries, 'kv', axis=0, tiled=True)  16.1 us
    add x15, other arithmetic, merge_partials(): out_first * jnp.repeat(weight_first, HEAD_WIDTH, axis=1)  14 us
    gather x1, local copies, waits for them, and re-layouts, on_device(): pair_values = returned[pair_slot]  10.2 us
    dot_general x1, matrix products, on_device(): jnp.einsum('scf,fd->scd', hidden, expert_down[0], preferred_element_type=...  9.57 us
  transfers between devices with their start and end apart: 2, of which 1 were waited for; matrix products, arithmetic and copies ran while one was open for 3% of the time, Pallas kernels for 0%

commit v1 on v0

v1 whole, which is shorter than its diff:
```python
import functools

import jax
import jax.numpy as jnp
from jax import lax
from jax.experimental import pallas as pl
from jax.experimental.pallas import tpu as pltpu
from jax.sharding import PartitionSpec as P

QUERY_HEADS = 24
KEY_VALUE_HEADS = 8
HEAD_WIDTH = 64
TOPK = 8
WINDOW = 4096
LANES = 128
HEAD_ROWS = 32

lowest = -1e30
MESH = pl.DeviceIdType.MESH


def silu_times(gate_part, up_part):
    return (gate_part / (1.0 + jnp.exp(-gate_part)) * up_part).astype(jnp.bfloat16)


def kernel(
    n,
    query_ref,
    bias_ref,
    sink_ref,
    decode_ref,
    prefill_ref,
    gain_ref,
    ids_ref,
    gates_ref,
    key_hbm,
    value_hbm,
    out_weight_hbm,
    expert_gate_hbm,
    expert_up_hbm,
    expert_down_hbm,
    out_ref,
    key,
    value,
    out_weight,
    expert_gate,
    expert_up,
    expert_down,
    own,
    tok,
    y,
    y_own,
    y_send,
    y_recv,
    sum_send,
    sum_recv,
    qbuf,
    scores,
    parts,
    parts_in,
    hidden,
    dec_out,
    dec_in,
    ret_out,
    ret_in,
    load_sem,
    tok_send_sem,
    tok_recv_sem,
    sib_send_sem,
    sib_recv_sem,
    y_send_sem,
    y_recv_sem,
    sum_send_sem,
    sum_recv_sem,
    q_sems,
    p_sems,
    d_sems,
    r_sems,
):
    chips = n // 2
    half_chips = chips // 2
    me = lax.axis_index("kv")
    core = me % 2
    chip = me // 2
    position = (1 - chip % 2) * (chip // 2) + (chip % 2) * (chips - 1 - chip // 2)

    def at_position(place):
        upper = place // half_chips
        return ((1 - upper) * 2 * place + upper * (2 * (chips - 1 - place) + 1)) * 2 + core

    right = at_position((position + 1) % chips)
    left = at_position((position + chips - 1) % chips)
    sibling = chip * 2 + 1 - core
    rows, width = own.shape
    half = rows // 2
    pieces = width // LANES

    loads = [
        pltpu.make_async_copy(a, b, load_sem.at[i])
        for i, (a, b) in enumerate(
            (
                (expert_gate_hbm, expert_gate),
                (expert_up_hbm, expert_up),
                (expert_down_hbm, expert_down),
                (key_hbm, key),
                (value_hbm, value),
                (out_weight_hbm, out_weight),
            )
        )
    ]
    for load in loads:
        load.start()

    barrier = pltpu.get_barrier_semaphore()

    def greet(k, _):
        pl.semaphore_signal(
            barrier, inc=1, device_id={"kv": (me + k) % n}, device_id_type=MESH
        )
        return 0

    lax.fori_loop(1, n, greet, 0)

    lane = lax.broadcasted_iota(jnp.int32, (rows, LANES), 1)
    row = lax.broadcasted_iota(jnp.int32, (rows, LANES), 0)
    gate_grid = jnp.zeros((rows, LANES), jnp.float32)
    for k in range(TOPK):
        gate_grid += jnp.where(ids_ref[:, k : k + 1] == lane % 64, gates_ref[:, k : k + 1], 0.0)
    dec_out[...] = jnp.zeros_like(dec_out)
    dec_out[pieces : pieces + 1, :] = gate_grid[rows - 1 : rows, :]
    gate_grid = jnp.where(row == rows - 1, 0.0, gate_grid)
    gate_high = gate_grid.astype(jnp.bfloat16).astype(jnp.float32)
    packed = jnp.where(lane < 64, gate_high, gate_grid - gate_high).astype(jnp.bfloat16)
    own[0 : rows - 1, :] = prefill_ref[...].astype(jnp.float32)
    own[rows - 1 : rows, :] = jnp.zeros((1, width), jnp.float32)
    for i in range(2):
        wide = own[i * half : (i + 1) * half, :]
        scale = lax.rsqrt(jnp.mean(wide * wide, axis=-1, keepdims=True) + 1e-06)
        tok[0, i, :, 0:width] = (wide * scale * gain_ref[...]).astype(jnp.bfloat16)
        tok[0, i, :, width : width + LANES] = packed[i * half : (i + 1) * half, :]
    qbuf[me] = query_ref[...]

    pl.semaphore_wait(barrier, n - 1)

    def exchange(source, target, sems):
        def copy(k):
            peer = (me + k) % n
            return pltpu.make_async_remote_copy(
                source(peer),
                target.at[me],
                sems.at[0, k],
                sems.at[1, me],
                device_id={"kv": peer},
                device_id_type=MESH,
            )

        def arrival(k):
            peer = (me + k) % n
            return pltpu.make_async_remote_copy(
                source(peer),
                target.at[peer],
                sems.at[0, k],
                sems.at[1, peer],
                device_id={"kv": peer},
                device_id_type=MESH,
            )

        def start():
            def one(k, _):
                copy(k).start()
                return 0

            lax.fori_loop(1, n, one, 0)

        def finish():
            def one(k, _):
                arrival(k).wait_recv()
                copy(k).wait_send()
                return 0

            lax.fori_loop(1, n, one, 0)

        return start, finish

    start_q, finish_q = exchange(lambda k: query_ref, qbuf, q_sems)
    start_p, finish_p = exchange(lambda k: parts.at[k, 0:QUERY_HEADS], parts_in, p_sems)
    start_d, finish_d = exchange(lambda k: dec_out, dec_in, d_sems)
    start_r, finish_r = exchange(lambda k: ret_out.at[k], ret_in, r_sems)

    def token_copy(s, way):
        return pltpu.make_async_remote_copy(
            tok.at[s, way],
            tok.at[s + 1, way],
            tok_send_sem.at[s, way],
            tok_recv_sem.at[s + 1, way],
            device_id={"kv": (right, left)[way]},
            device_id_type=MESH,
        )

    def sibling_copy(s):
        return pltpu.make_async_remote_copy(
            tok.at[s, 0:2],
            tok.at[s, 2:4],
            sib_send_sem.at[s],
            sib_recv_sem.at[s],
            device_id={"kv": sibling},
            device_id_type=MESH,
        )

    def y_copy(s):
        return pltpu.make_async_remote_copy(
            y_send.at[s % 2],
            y_recv.at[s],
            y_send_sem.at[s],
            y_recv_sem.at[s],
            device_id={"kv": sibling},
            device_id_type=MESH,
        )

    def sum_copy(s, way):
        return pltpu.make_async_remote_copy(
            sum_send.at[s % 2, way],
            sum_recv.at[s, way],
            sum_send_sem.at[s, way],
            sum_recv_sem.at[s, way],
            device_id={"kv": (right, left)[way]},
            device_id_type=MESH,
        )

    def attend():
        finish_q()
        loads[3].wait()
        loads[4].wait()
        columns = KEY_VALUE_HEADS * HEAD_WIDTH
        count = n * HEAD_ROWS
        spread = (
            lax.broadcasted_iota(jnp.int32, (LANES, columns), 0)
            == lax.broadcasted_iota(jnp.int32, (LANES, columns), 1) % HEAD_WIDTH
        ).astype(jnp.float32).astype(jnp.bfloat16)
        group = QUERY_HEADS // KEY_VALUE_HEADS
        head = lax.broadcasted_iota(jnp.int32, (count, columns), 0) % HEAD_ROWS
        column = lax.broadcasted_iota(jnp.int32, (count, columns), 1)
        belongs = head // group == column // HEAD_WIDTH
        queries = qbuf[...].reshape(count, LANES)
        queries = jnp.dot(queries, spread, preferred_element_type=jnp.float32)
        queries = jnp.where(belongs, queries * HEAD_WIDTH**-0.5, 0.0).astype(jnp.bfloat16)
        scores[...] = lax.dot_general(
            queries, key[...], (((1,), (1,)), ((), ())), preferred_element_type=jnp.float32
        )
        lanes = lax.broadcasted_iota(jnp.int32, (HEAD_ROWS, LANES), 1)
        heads = lax.broadcasted_iota(jnp.int32, (HEAD_ROWS, LANES), 0)

        def per_request(r, _):
            at = pl.ds(pl.multiple_of(r * HEAD_ROWS, HEAD_ROWS), HEAD_ROWS)
            allowed = bias_ref[r] > 0.5
            score = jnp.where(allowed, scores[at, :], lowest)
            top = jnp.max(score, axis=-1, keepdims=True)
            weight = jnp.where(allowed, jnp.exp(score - top), 0.0)
            weight = weight.astype(jnp.bfloat16).astype(jnp.float32)
            total = jnp.sum(weight, axis=-1, keepdims=True)
            scores[at, :] = weight
            parts[r] = jnp.where(lanes % 64 < 32, top, total)
            return 0

        lax.fori_loop(0, n, per_request, 0)
        out = jnp.dot(
            scores[...].astype(jnp.bfloat16), value[...], preferred_element_type=jnp.float32
        )
        out = jnp.where(belongs, out, 0.0)
        folded = out[:, 0:LANES]
        for j in range(1, columns // LANES):
            folded += out[:, j * LANES : (j + 1) * LANES]
        in_half = (heads // group) % 2 == lanes // 64
        parts[...] = jnp.where(in_half[None], folded.reshape(n, HEAD_ROWS, LANES), parts[...])
        parts_in[me] = parts[me, 0:QUERY_HEADS]
        start_p()

    def project():
        finish_p()
        loads[5].wait()
        group = QUERY_HEADS // KEY_VALUE_HEADS
        lanes = lax.broadcasted_iota(jnp.int32, (QUERY_HEADS, LANES), 1)
        heads = lax.broadcasted_iota(jnp.int32, (QUERY_HEADS, LANES), 0)
        in_half = (heads // group) % 2 == lanes // 64
        is_top = jnp.logical_not(in_half) & (lanes % 64 < 32)
        is_total = jnp.logical_not(in_half) & (lanes % 64 >= 32)
        every = parts_in[...]
        tops = jnp.max(jnp.where(is_top[None], every, -3e38), axis=-1, keepdims=True)
        totals = jnp.max(jnp.where(is_total[None], every, -1.0), axis=-1, keepdims=True)
        top = jnp.max(tops, axis=0)
        share = jnp.exp(tops - top[None])
        total = jnp.sum(share * totals, axis=0)
        out = jnp.sum(share * every, axis=0)
        sink = sink_ref[...]
        ceiling = jnp.maximum(top, sink)
        keep = jnp.exp(top - ceiling)
        attended = out * (keep / (total * keep + jnp.exp(sink - ceiling)))
        attended = jnp.where(in_half, attended, 0.0)
        attended = attended + pltpu.roll(attended, 64, 1)
        low = lax.broadcasted_iota(jnp.int32, (1, LANES), 1) < 64
        line = jnp.concatenate(
            [
                jnp.where(low, attended[2 * j : 2 * j + 1, :], attended[2 * j + 1 : 2 * j + 2, :])
                for j in range(QUERY_HEADS // 2)
            ],
            axis=1,
        )
        line = jnp.broadcast_to(line, (16, line.shape[1])).astype(jnp.bfloat16)
        projected = jnp.dot(line, out_weight[...], preferred_element_type=jnp.float32)
        stream = (decode_ref[...].astype(jnp.float32) + projected[0:1, :]).astype(jnp.bfloat16)
        stream = stream.astype(jnp.float32)
        hidden[...] = stream
        scale = lax.rsqrt(jnp.mean(stream * stream, axis=-1, keepdims=True) + 1e-06)
        normed = stream * scale * gain_ref[...]
        for j in range(pieces):
            dec_out[j : j + 1, :] = normed[:, j * LANES : (j + 1) * LANES]
        dec_in[me] = dec_out[...]
        start_d()

    def decode_expert():
        finish_d()
        x = jnp.concatenate([dec_in[:, j, :] for j in range(pieces)], axis=1).astype(jnp.bfloat16)
        lanes = lax.broadcasted_iota(jnp.int32, (n, LANES), 1)
        weight = jnp.sum(
            jnp.where(lanes == me, dec_in[:, pieces, :], 0.0), axis=-1, keepdims=True
        )
        h = silu_times(
            jnp.dot(x, expert_gate[...], preferred_element_type=jnp.float32),
            jnp.dot(x, expert_up[...], preferred_element_type=jnp.float32),
        )
        made = jnp.dot(h, expert_down[...], preferred_element_type=jnp.float32) * weight
        ret_out[...] = jnp.zeros_like(ret_out)
        for j in range(pieces):
            ret_out[:, j, :] = made[:, j * LANES : (j + 1) * LANES]
        ret_in[me] = ret_out[me]
        start_r()

    def step(s, _):
        @pl.when(s >= 1)
        def _():
            token_copy(s - 1, 0).wait_recv()
            token_copy(s - 1, 1).wait_recv()

        @pl.when(s < chips - 1)
        def _():
            token_copy(s, 0).start()
            token_copy(s, 1).start()

        sibling_copy(s).start()

        @pl.when(s == 0)
        def _():
            start_q()
            for load in loads[:3]:
                load.wait()

        sibling_copy(s).wait_recv()
        x = tok[s].reshape(4 * half, width + LANES)
        lanes = lax.broadcasted_iota(jnp.int32, (4 * half, LANES), 1)
        weight = jnp.sum(
            jnp.where(lanes % 64 == me, x[:, width:].astype(jnp.float32), 0.0),
            axis=-1,
            keepdims=True,
        )
        x = x[:, 0:width]
        h = silu_times(
            jnp.dot(x, expert_gate[...], preferred_element_type=jnp.float32),
            jnp.dot(x, expert_up[...], preferred_element_type=jnp.float32),
        )
        y[...] = jnp.dot(h, expert_down[...], preferred_element_type=jnp.float32) * weight

        @pl.when(s >= 2)
        def _():
            y_copy(s - 2).wait_send()

        y_send[s % 2] = y[rows : 2 * rows, :].astype(jnp.bfloat16)
        y_copy(s).start()

        @pl.when(s == 1)
        def _():
            attend()

        @pl.when(s == chips // 2 - 1)
        def _():
            project()

        @pl.when(s == chips // 2 + 1)
        def _():
            decode_expert()

        y_copy(s).wait_recv()
        summed = y[0:rows, :] + y_recv[s].astype(jnp.float32)

        @pl.when(s == 0)
        def _():
            y_own[...] = summed

        @pl.when(s >= 1)
        def _():
            y[0:rows, :] = summed

        @pl.when(s >= 2)
        def _():
            for way in range(2):
                sum_copy(s - 1, way).wait_recv()
                at = slice(way * half, (way + 1) * half)
                y[at, :] = y[at, :] + sum_recv[s - 1, way].astype(jnp.float32)

        @pl.when(s >= 3)
        def _():
            sum_copy(s - 2, 0).wait_send()
            sum_copy(s - 2, 1).wait_send()

        @pl.when(s >= 1)
        def _():
            for way in range(2):
                at = slice(way * half, (way + 1) * half)
                sum_send[s % 2, way] = y[at, :].astype(jnp.bfloat16)
                sum_copy(s, way).start()

        return 0

    lax.fori_loop(0, chips, step, 0)

    last = chips - 1
    finish_r()
    line = jnp.sum(ret_in[...], axis=0)
    line = jnp.concatenate([line[j : j + 1, :] for j in range(pieces)], axis=1)
    line = line + hidden[...]
    for way in range(2):
        sum_copy(last, way).wait_recv()
        at = slice(way * half, (way + 1) * half)
        made = own[at, :] + y_own[at, :] + sum_recv[last, way].astype(jnp.float32)
        if way == 1:
            place = lax.broadcasted_iota(jnp.int32, (half, width), 0)
            made = jnp.where(place == half - 1, line, made)
        out_ref[at, :] = made.astype(jnp.bfloat16)

    def drain(s, _):
        token_copy(s, 0).wait_send()
        token_copy(s, 1).wait_send()
        return 0

    lax.fori_loop(0, chips - 1, drain, 0)

    def drain_sibling(s, _):
        sibling_copy(s).wait_send()
        return 0

    lax.fori_loop(0, chips, drain_sibling, 0)
    for s in (last - 1, last):
        y_copy(s).wait_send()
        for way in range(2):
            sum_copy(s, way).wait_send()


def on_device(
    queries,
    key_cache_pages,
    value_cache_pages,
    page_table,
    lengths,
    sink_head_logits,
    output_weight,
    decode_stream,
    prefill_stream,
    norm_gain,
    expert_gate,
    expert_up,
    expert_down,
    route_ids,
    route_gates,
):
    n = lax.axis_size("kv")
    chips = n // 2
    device_index = lax.axis_index(("ep", "kv"))
    pool, page_length, columns = key_cache_pages.shape
    rows = route_ids.shape[0]
    half = rows // 2
    width = prefill_stream.shape[1]
    hidden_units = expert_gate.shape[2]
    first = lax.axis_index("ep") * n
    table = lax.dynamic_slice_in_dim(page_table, first, n, 0)
    length = lax.dynamic_slice_in_dim(lengths, first, n, 0)
    begin = jnp.maximum(length - WINDOW, 0)
    first_page = begin // page_length
    slot = first_page[:, None] + jnp.arange(page_table.shape[1], dtype=jnp.int32)[None, :]
    live = slot * page_length < length[:, None]
    local = jnp.where(live, table - device_index * pool, -1)
    hit = local[:, None, :] == jnp.arange(pool, dtype=jnp.int32)[None, :, None]
    page = jnp.max(jnp.where(hit, slot[:, None, :], -1), axis=-1)
    where = page[:, :, None] * page_length + jnp.arange(page_length, dtype=jnp.int32)
    inside = (where >= begin[:, None, None]) & (where < length[:, None, None]) & (where >= 0)
    allowed = inside.astype(jnp.float32).reshape(n, 1, pool * page_length)
    query = jnp.pad(
        queries.reshape(QUERY_HEADS, HEAD_WIDTH),
        ((0, HEAD_ROWS - QUERY_HEADS), (0, LANES - HEAD_WIDTH)),
    )
    bf16, f32 = jnp.bfloat16, jnp.float32
    vmem = pl.BlockSpec(memory_space=pltpu.VMEM)
    hbm = pl.BlockSpec(memory_space=pl.ANY)
    dma = pltpu.SemaphoreType.DMA
    return pl.pallas_call(
        functools.partial(kernel, n),
        out_shape=jax.ShapeDtypeStruct((rows, width), bf16),
        in_specs=[vmem] * 8 + [hbm] * 6,
        out_specs=vmem,
        scratch_shapes=[
            pltpu.VMEM((pool * page_length, columns), bf16),
            pltpu.VMEM((pool * page_length, columns), bf16),
            pltpu.VMEM(output_weight.shape, bf16),
            pltpu.VMEM((width, hidden_units), bf16),
            pltpu.VMEM((width, hidden_units), bf16),
            pltpu.VMEM((hidden_units, width), bf16),
            pltpu.VMEM((rows, width), f32),
            pltpu.VMEM((chips, 4, half, width + LANES), bf16),
            pltpu.VMEM((2 * rows, width), f32),
            pltpu.VMEM((rows, width), f32),
            pltpu.VMEM((2, rows, width), bf16),
            pltpu.VMEM((chips, rows, width), bf16),
            pltpu.VMEM((2, 2, half, width), bf16),
            pltpu.VMEM((chips, 2, half, width), bf16),
            pltpu.VMEM((n, HEAD_ROWS, LANES), bf16),
            pltpu.VMEM((n * HEAD_ROWS, pool * page_length), f32),
            pltpu.VMEM((n, HEAD_ROWS, LANES), f32),
            pltpu.VMEM((n, QUERY_HEADS, LANES), f32),
            pltpu.VMEM((1, width), f32),
            pltpu.VMEM((16, LANES), f32),
            pltpu.VMEM((n, 16, LANES), f32),
            pltpu.VMEM((n, 16, LANES), f32),
            pltpu.VMEM((n, 16, LANES), f32),
            dma((6,)),
            dma((chips, 2)),
            dma((chips, 2)),
            dma((chips,)),
            dma((chips,)),
            dma((chips,)),
            dma((chips,)),
            dma((chips, 2)),
            dma((chips, 2)),
            dma((2, n)),
            dma((2, n)),
            dma((2, n)),
            dma((2, n)),
        ],
        compiler_params=pltpu.CompilerParams(
            collective_id=0, has_side_effects=True, vmem_limit_bytes=60 * 1024 * 1024
        ),
    )(
        query,
        allowed,
        sink_head_logits[:, None],
        decode_stream,
        prefill_stream,
        norm_gain[None, :],
        route_ids,
        route_gates,
        key_cache_pages.reshape(pool * page_length, columns),
        value_cache_pages.reshape(pool * page_length, columns),
        output_weight,
        expert_gate[0],
        expert_up[0],
        expert_down[0],
    )


def solution(mesh):
    in_specs = (
        P(("ep", "kv"), None),
        P(("ep", "kv"), None, None),
        P(("ep", "kv"), None, None),
        P(),
        P(),
        P(),
        P(),
        P(("ep", "kv"), None),
        P(("ep", "kv"), None),
        P(),
        P("kv", None, None),
        P("kv", None, None),
        P("kv", None, None),
        P(("ep", "kv"), None),
        P(("ep", "kv"), None),
    )
    out_specs = P(("ep", "kv"), None)
    return jax.shard_map(
        on_device, mesh=mesh, in_specs=in_specs, out_specs=out_specs, check_vma=False
    )
```

time: 397 us -> 102 us (0.26)
  the two profiles are of different devices: /device:TPU:13 before, /device:TPU:0 now
where the time goes in v1:
time: 102 us
  Pallas kernels  90.4 us (89%)
  local copies, waits for them, and re-layouts  8.18 us (8%)
  other arithmetic  3.39 us (3%)
    pallas_call x1, Pallas kernels, on_device(): pl.pallas_call(functools.partial(kernel, n), out_shape=jax.ShapeDtypeStru...  90.4 us
    unnamed x3, local copies, waits for them, and re-layouts  4.57 us

profile of v1, /device:TPU:0, one launch (start us, length us, event | category | flops | bytes accessed | tf_op | source)
XLA Modules:
  0.0 102.0 jit_solution(4508899301295019896)
XLA Ops:
  0.0 0.7 add_maximum_fusion
  0.7 0.7 reduce
  1.5 0.1 reshape.110
  1.6 0.6 pad.4.query_ref
  2.2 1.3 %broadcast_in_dim.36.gain_ref = f32[1,1536]{1,0:T(1,128)} reshape(f32[1536]{0:T(1024)} %param.24) | data formatting | bytes 12288 | tf_op jit(solution)/shard_map/broadcast_in_dim | solution.py:555
  3.5 0.1 add.62
  3.5 1.3 %copy.23.sink_ref = f32[24,1]{1,0:T(8,128)} copy(f32[24,1]{0,1:T(1,128)} %bitcast.11) | data formatting | bytes 192 | tf_op jit(solution)/shard_map/broadcast_in_dim | solution.py:552
  4.9 0.8 subtract_select_fusion
  5.6 0.3 select_reduce_fusion
  6.0 1.4 %copy.24.ids_ref = s32[128,8]{1,0:T(8,128)} copy(s32[128,8]{0,1:T(8,128)} %param.28) | data formatting | bytes 8192 | tf_op args[13]
  7.4 1.4 %copy.25.gates_ref = f32[128,8]{1,0:T(8,128)} copy(f32[128,8]{0,1:T(8,128)} %param.29) | data formatting | bytes 8192 | tf_op args[14]
  8.8 0.1 add.59
  8.9 0.1 add.60
  9.0 0.8 and_convert_fusion.bias_ref
  9.8 90.4 %shard_map.145 = bf16[128,1536]{1,0:T(8,128)(2,1)} custom-call(bf16[32,128]{1,0:T(8,128)(2,1)} %pad.4.query_ref, f32[16,1,1024]{2,1,0:T(1,128)} %and_convert_fusion.bias_ref, f32[24,1]{1,0:T(8,128)} %copy.23.sink_ref, bf16[1,1536]{1,0:T(2,128)(2,1)} %decode_ref.1, bf16[127,1536]{1,0:T(8,128)(2,1)} %prefill_ref.1, f32[1,1536]{1,0:T(1,128)} %broadcast_in_dim.36.gain_ref, ...), custom_call_target="tpu_custom_call" | custom-call | tf_op jit(solution)/shard_map/pallas_call | solution.py:503
  100.3 1.8 %copy.27 = bf16[128,1536]{1,0:T(8,128)(2,1)} copy(bf16[128,1536]{1,0:T(8,128)(2,1)} %shard_map.145) | data formatting | bytes 786432
  (3 shorter events, 0.0 us)

commit v2 on v1

--- a/solution.py
+++ b/solution.py
@@ -25,8 +25,10 @@
 
 def kernel(
     n,
+    page_length,
     query_ref,
-    bias_ref,
+    table_ref,
+    length_ref,
     sink_ref,
     decode_ref,
     prefill_ref,
@@ -54,6 +56,8 @@
     y_recv,
     sum_send,
     sum_recv,
+    qown,
+    bias,
     qbuf,
     scores,
     parts,
@@ -123,9 +127,12 @@
 
     lane = lax.broadcasted_iota(jnp.int32, (rows, LANES), 1)
     row = lax.broadcasted_iota(jnp.int32, (rows, LANES), 0)
-    gate_grid = jnp.zeros((rows, LANES), jnp.float32)
+    expert_row = lax.broadcasted_iota(jnp.int32, (LANES, rows), 0) % 64
+    gate_grid = jnp.zeros((LANES, rows), jnp.float32)
     for k in range(TOPK):
-        gate_grid += jnp.where(ids_ref[:, k : k + 1] == lane % 64, gates_ref[:, k : k + 1], 0.0)
+        gate_grid += jnp.where(ids_ref[k : k + 1, :] == expert_row, gates_ref[k : k + 1, :], 0.0)
+    gate_grid = gate_grid.T
+    gain = jnp.concatenate([gain_ref[j : j + 1, :] for j in range(pieces)], axis=1)
     dec_out[...] = jnp.zeros_like(dec_out)
     dec_out[pieces : pieces + 1, :] = gate_grid[rows - 1 : rows, :]
     gate_grid = jnp.where(row == rows - 1, 0.0, gate_grid)
@@ -136,9 +143,18 @@
     for i in range(2):
         wide = own[i * half : (i + 1) * half, :]
         scale = lax.rsqrt(jnp.mean(wide * wide, axis=-1, keepdims=True) + 1e-06)
-        tok[0, i, :, 0:width] = (wide * scale * gain_ref[...]).astype(jnp.bfloat16)
+        tok[0, i, :, 0:width] = (wide * scale * gain).astype(jnp.bfloat16)
         tok[0, i, :, width : width + LANES] = packed[i * half : (i + 1) * half, :]
-    qbuf[me] = query_ref[...]
+    wide_query = query_ref[...].astype(jnp.float32)
+    for h in range(QUERY_HEADS):
+        line = wide_query[:, h // 2 * LANES : h // 2 * LANES + LANES]
+        qown_row = pltpu.roll(line, 64, 1) if h % 2 else line
+        scores[h : h + 1, 0:LANES] = qown_row
+    scores[QUERY_HEADS:HEAD_ROWS, 0:LANES] = jnp.zeros(
+        (HEAD_ROWS - QUERY_HEADS, LANES), jnp.float32
+    )
+    qown[...] = scores[0:HEAD_ROWS, 0:LANES].astype(jnp.bfloat16)
+    qbuf[me] = qown[...]
 
     pl.semaphore_wait(barrier, n - 1)
 
@@ -182,7 +198,7 @@
 
         return start, finish
 
-    start_q, finish_q = exchange(lambda k: query_ref, qbuf, q_sems)
+    start_q, finish_q = exchange(lambda k: qown, qbuf, q_sems)
     start_p, finish_p = exchange(lambda k: parts.at[k, 0:QUERY_HEADS], parts_in, p_sems)
     start_d, finish_d = exchange(lambda k: dec_out, dec_in, d_sems)
     start_r, finish_r = exchange(lambda k: ret_out.at[k], ret_in, r_sems)
@@ -227,7 +243,33 @@
             device_id_type=MESH,
         )
 
+    def window_mask():
+        requests, slots = table_ref.shape
+        first = lax.axis_index("ep") * n
+        pool = key.shape[0] // page_length
+        across = lax.broadcasted_iota(jnp.int32, (n, requests), 1)
+        down = lax.broadcasted_iota(jnp.int32, (n, requests), 0)
+        length = jnp.sum(
+            jnp.where(across == first + down, length_ref[...], 0), axis=-1, keepdims=True
+        )
+        begin = jnp.maximum(length - WINDOW, 0)
+        slot = begin // page_length + lax.broadcasted_iota(jnp.int32, (n, slots), 1)
+        table = table_ref[pl.ds(pl.multiple_of(first, 8), n), :]
+        local = jnp.where(slot * page_length < length, table - (first + me) * pool, -1)
+        lanes = lax.broadcasted_iota(jnp.int32, (n, LANES), 1)
+        per = LANES // page_length
+        for j in range(pool // per):
+            page = jnp.full((n, LANES), -1, jnp.int32)
+            for i in range(per):
+                hit = jnp.where(local == j * per + i, slot, -1)
+                held = jnp.max(hit, axis=-1, keepdims=True)
+                page = jnp.where(lanes // page_length == i, held, page)
+            place = page * page_length + lanes % page_length
+            inside = (page >= 0) & (place >= begin) & (place < length)
+            bias[:, j * LANES : (j + 1) * LANES] = jnp.where(inside, 1.0, 0.0)
+
     def attend():
+        window_mask()
         finish_q()
         loads[3].wait()
         loads[4].wait()
@@ -252,7 +294,7 @@
 
         def per_request(r, _):
             at = pl.ds(pl.multiple_of(r * HEAD_ROWS, HEAD_ROWS), HEAD_ROWS)
-            allowed = bias_ref[r] > 0.5
+            allowed = bias[pl.ds(r, 1), :] > 0.5
             score = jnp.where(allowed, scores[at, :], lowest)
             top = jnp.max(score, axis=-1, keepdims=True)
             weight = jnp.where(allowed, jnp.exp(score - top), 0.0)
@@ -291,7 +333,9 @@
         share = jnp.exp(tops - top[None])
         total = jnp.sum(share * totals, axis=0)
         out = jnp.sum(share * every, axis=0)
-        sink = sink_ref[...]
+        across = lax.broadcasted_iota(jnp.int32, (QUERY_HEADS, QUERY_HEADS), 1)
+        down = lax.broadcasted_iota(jnp.int32, (QUERY_HEADS, QUERY_HEADS), 0)
+        sink = jnp.sum(jnp.where(across == down, sink_ref[...], 0.0), axis=-1, keepdims=True)
         ceiling = jnp.maximum(top, sink)
         keep = jnp.exp(top - ceiling)
         attended = out * (keep / (total * keep + jnp.exp(sink - ceiling)))
@@ -311,7 +355,7 @@
         stream = stream.astype(jnp.float32)
         hidden[...] = stream
         scale = lax.rsqrt(jnp.mean(stream * stream, axis=-1, keepdims=True) + 1e-06)
-        normed = stream * scale * gain_ref[...]
+        normed = stream * scale * gain
         for j in range(pieces):
             dec_out[j : j + 1, :] = normed[:, j * LANES : (j + 1) * LANES]
         dec_in[me] = dec_out[...]
@@ -336,23 +380,17 @@
         start_r()
 
     def step(s, _):
-        @pl.when(s >= 1)
-        def _():
-            token_copy(s - 1, 0).wait_recv()
-            token_copy(s - 1, 1).wait_recv()
-
-        @pl.when(s < chips - 1)
-        def _():
-            token_copy(s, 0).start()
-            token_copy(s, 1).start()
-
-        sibling_copy(s).start()
-
-        @pl.when(s == 0)
-        def _():
-            start_q()
-            for load in loads[:3]:
-                load.wait()
+        @pl.when((s < chips - 1) & (s > 0))
+        def _():
+            token_copy(s, 0).wait_recv()
+            token_copy(s, 1).wait_recv()
+
+            @pl.when(s < chips - 2)
+            def _():
+                token_copy(s + 1, 0).start()
+                token_copy(s + 1, 1).start()
+
+            sibling_copy(s + 1).start()
 
         sibling_copy(s).wait_recv()
         x = tok[s].reshape(4 * half, width + LANES)
@@ -376,15 +414,27 @@
         y_send[s % 2] = y[rows : 2 * rows, :].astype(jnp.bfloat16)
         y_copy(s).start()
 
-        @pl.when(s == 1)
+        @pl.when(s == 0)
+        def _():
+            token_copy(s, 0).wait_recv()
+            token_copy(s, 1).wait_recv()
+
+            @pl.when(s < chips - 2)
+            def _():
+                token_copy(s + 1, 0).start()
+                token_copy(s + 1, 1).start()
+
+            sibling_copy(s + 1).start()
+
+        @pl.when(s == 0)
         def _():
             attend()
 
-        @pl.when(s == chips // 2 - 1)
+        @pl.when(s == chips // 4)
         def _():
             project()
 
-        @pl.when(s == chips // 2 + 1)
+        @pl.when(s == chips // 2)
         def _():
             decode_expert()
 
@@ -420,6 +470,12 @@
 
         return 0
 
+    for way in range(2):
+        token_copy(0, way).start()
+    sibling_copy(0).start()
+    start_q()
+    for load in loads[:3]:
+        load.wait()
     lax.fori_loop(0, chips, step, 0)
 
     last = chips - 1
@@ -473,37 +529,19 @@
 ):
     n = lax.axis_size("kv")
     chips = n // 2
-    device_index = lax.axis_index(("ep", "kv"))
     pool, page_length, columns = key_cache_pages.shape
     rows = route_ids.shape[0]
     half = rows // 2
     width = prefill_stream.shape[1]
     hidden_units = expert_gate.shape[2]
-    first = lax.axis_index("ep") * n
-    table = lax.dynamic_slice_in_dim(page_table, first, n, 0)
-    length = lax.dynamic_slice_in_dim(lengths, first, n, 0)
-    begin = jnp.maximum(length - WINDOW, 0)
-    first_page = begin // page_length
-    slot = first_page[:, None] + jnp.arange(page_table.shape[1], dtype=jnp.int32)[None, :]
-    live = slot * page_length < length[:, None]
-    local = jnp.where(live, table - device_index * pool, -1)
-    hit = local[:, None, :] == jnp.arange(pool, dtype=jnp.int32)[None, :, None]
-    page = jnp.max(jnp.where(hit, slot[:, None, :], -1), axis=-1)
-    where = page[:, :, None] * page_length + jnp.arange(page_length, dtype=jnp.int32)
-    inside = (where >= begin[:, None, None]) & (where < length[:, None, None]) & (where >= 0)
-    allowed = inside.astype(jnp.float32).reshape(n, 1, pool * page_length)
-    query = jnp.pad(
-        queries.reshape(QUERY_HEADS, HEAD_WIDTH),
-        ((0, HEAD_ROWS - QUERY_HEADS), (0, LANES - HEAD_WIDTH)),
-    )
     bf16, f32 = jnp.bfloat16, jnp.float32
     vmem = pl.BlockSpec(memory_space=pltpu.VMEM)
     hbm = pl.BlockSpec(memory_space=pl.ANY)
     dma = pltpu.SemaphoreType.DMA
     return pl.pallas_call(
-        functools.partial(kernel, n),
+        functools.partial(kernel, n, page_length),
         out_shape=jax.ShapeDtypeStruct((rows, width), bf16),
-        in_specs=[vmem] * 8 + [hbm] * 6,
+        in_specs=[vmem] * 9 + [hbm] * 6,
         out_specs=vmem,
         scratch_shapes=[
             pltpu.VMEM((pool * page_length, columns), bf16),
@@ -520,6 +558,8 @@
             pltpu.VMEM((chips, rows, width), bf16),
             pltpu.VMEM((2, 2, half, width), bf16),
             pltpu.VMEM((chips, 2, half, width), bf16),
+            pltpu.VMEM((HEAD_ROWS, LANES), bf16),
+            pltpu.VMEM((n, pool * page_length), f32),
             pltpu.VMEM((n, HEAD_ROWS, LANES), bf16),
             pltpu.VMEM((n * HEAD_ROWS, pool * page_length), f32),
             pltpu.VMEM((n, HEAD_ROWS, LANES), f32),
@@ -547,14 +587,15 @@
             collective_id=0, has_side_effects=True, vmem_limit_bytes=60 * 1024 * 1024
         ),
     )(
-        query,
-        allowed,
-        sink_head_logits[:, None],
+        queries,
+        page_table,
+        lengths[None, :],
+        sink_head_logits[None, :],
         decode_stream,
         prefill_stream,
-        norm_gain[None, :],
-        route_ids,
-        route_gates,
+        norm_gain.reshape(width // LANES, LANES),
+        route_ids.T,
+        route_gates.T,
         key_cache_pages.reshape(pool * page_length, columns),
         value_cache_pages.reshape(pool * page_length, columns),
         output_weight,

time: 102 us -> 93 us (0.912)
  local copies, waits for them, and re-layouts: 8.18 us -> 1.77 us
  other arithmetic: 3.39 us -> 0 us
    unnamed x3 -> x1, local copies, waits for them, and re-layouts: 4.57 us -> 1.77 us
    broadcast_in_dim x2 -> x0, local copies, waits for them, and re-layouts: 2.62 us -> none  [the longest x1 1.33 us: on_device(): sink_head_logits[:, None]]
where the time goes in v2:
time: 93 us; the launch traced here: 92.9 us
  Pallas kernels  91.1 us (98%)
  local copies, waits for them, and re-layouts  1.77 us (2%)
    pallas_call x1, Pallas kernels, on_device(): pl.pallas_call(functools.partial(kernel, n, page_length), out_shape=jax.S...  91.1 us

profile of v2, /device:TPU:0, one launch (start us, length us, event | category | flops | bytes accessed | tf_op | source)
XLA Modules:
  0.0 92.9 jit_solution(12418301428489590500)
XLA Ops:
  0.0 91.1 %shard_map.145 = bf16[128,1536]{1,0:T(8,128)(2,1)} custom-call(bf16[1,1536]{1,0:T(2,128)(2,1)} %query_ref.1, s32[32,65]{1,0:T(8,128)} %table_ref.1, s32[1,32]{1,0:T(1,128)} %bitcast.18, f32[1,24]{1,0:T(1,128)} %bitcast.19, bf16[1,1536]{1,0:T(2,128)(2,1)} %decode_ref.1, bf16[127,1536]{1,0:T(8,128)(2,1)} %prefill_ref.1, f32[12,128]{1,0:T(8,128)} %bitcast.15, ...), custom_call_target="tpu_custom_call" | custom-call | tf_op jit(solution)/shard_map/pallas_call | solution.py:541
  91.1 1.8 %copy.17 = bf16[128,1536]{1,0:T(8,128)(2,1)} copy(bf16[128,1536]{1,0:T(8,128)(2,1)} %shard_map.145) | data formatting | bytes 786432

commit v3 on v2

--- a/solution.py
+++ b/solution.py
@@ -430,11 +430,11 @@
         def _():
             attend()
 
-        @pl.when(s == chips // 4)
+        @pl.when(s == chips // 2 - 1)
         def _():
             project()
 
-        @pl.when(s == chips // 2)
+        @pl.when(s == chips - 2)
         def _():
             decode_expert()
 
@@ -470,10 +470,10 @@
 
         return 0
 
+    start_q()
     for way in range(2):
         token_copy(0, way).start()
     sibling_copy(0).start()
-    start_q()
     for load in loads[:3]:
         load.wait()
     lax.fori_loop(0, chips, step, 0)

time: 93 us -> 90 us (0.968)
  Pallas kernels: 91.1 us -> 88.1 us
    pallas_call x1, Pallas kernels: 91.1 us -> 88.1 us  [on_device(): pl.pallas_call(functools.partial(kernel, n, page_length), out_shape=jax.S...]
where the time goes in v3:
time: 90 us; the launch traced here: 89.9 us
  Pallas kernels  88.1 us (98%)
  local copies, waits for them, and re-layouts  1.77 us (2%)
    pallas_call x1, Pallas kernels, on_device(): pl.pallas_call(functools.partial(kernel, n, page_length), out_shape=jax.S...  88.1 us

profile of v3, /device:TPU:0, one launch (start us, length us, event | category | flops | bytes accessed | tf_op | source)
XLA Modules:
  0.0 89.9 jit_solution(3599967046033199193)
XLA Ops:
  0.0 88.1 %shard_map.145 = bf16[128,1536]{1,0:T(8,128)(2,1)} custom-call(bf16[1,1536]{1,0:T(2,128)(2,1)} %query_ref.1, s32[32,65]{1,0:T(8,128)} %table_ref.1, s32[1,32]{1,0:T(1,128)} %bitcast.18, f32[1,24]{1,0:T(1,128)} %bitcast.19, bf16[1,1536]{1,0:T(2,128)(2,1)} %decode_ref.1, bf16[127,1536]{1,0:T(8,128)(2,1)} %prefill_ref.1, f32[12,128]{1,0:T(8,128)} %bitcast.15, ...), custom_call_target="tpu_custom_call" | custom-call | tf_op jit(solution)/shard_map/pallas_call | solution.py:541
  88.1 1.8 %copy.17 = bf16[128,1536]{1,0:T(8,128)(2,1)} copy(bf16[128,1536]{1,0:T(8,128)(2,1)} %shard_map.145) | data formatting | bytes 786432
